TPU v7x, 32 devices: a whole 2x2x4 slice. The times are simulated.
32 devices in a mesh: seq: 8 (over z, core), head: 4 (over y, x).
Axes of the slice: x: 2, y: 2, z: 4, core: 2. Of those that a mesh axis runs over, the one named last changes fastest.
Arguments:
- query_rows: bfloat16 [5120, 8192], P(('seq', 'head')), may hold values from -6 to 6
- rotated_key_rows: bfloat16 [5120, 1024], P(('seq', 'head')), may hold values from -6 to 6
- value_row_matrix: bfloat16 [5120, 1024], P(('seq', 'head')), may hold values from -6 to 6
- group_assign: int32 [64], replicated, may hold values from 0 to 63, each once
- vertical_blocks: int32 [64, 4], replicated, may hold values from 0 to 39
- slash_offsets: int32 [64, 3], replicated, may hold values from 0 to 5, as said below
Outputs:
- attended: bfloat16 [5120, 8192], P(('seq', 'head'))
Inputs may be any that keep to these rules, and one draw needn't show every extreme that they name: `slash_offsets`: each head's first offset is 0 and its offsets are distinct.
All inputs are finite; a program needn't handle non-finite values.
Results may differ from a plain program's by a relative error of at most 0.0045.
Values may be sent and summed in bfloat16 or wider, within the bound.
A program may use at most 64 MiB of HBM per device.

v0:
```python
import math

import jax
import jax.numpy as jnp
from jax import lax
from jax.sharding import PartitionSpec as P

QUERY_HEADS = 64
KEY_VALUE_HEADS = 8
HEAD_SIZE = 128
BLOCK_TOKENS = 128
NV = 4


def passed_along(value, axis, steps):
    count = lax.axis_size(axis)
    leading, last = (max(0, -steps), min(count, count - steps))
    return lax.ppermute(value, axis, [(source, source + steps) for source in range(leading, last)])


def per_device(
    query_rows, rotated_key_rows, value_row_matrix, group_assign, vertical_blocks, slash_offsets
):
    groups = lax.axis_size("head")
    slot_count = QUERY_HEADS // groups
    sharing_count = QUERY_HEADS // KEY_VALUE_HEADS
    resident_rows = query_rows.shape[0]
    key_value_heads = group_assign // sharing_count
    query_sel = query_rows.reshape(resident_rows, QUERY_HEADS, HEAD_SIZE)[:, group_assign]
    selected_keys = rotated_key_rows.reshape(resident_rows, KEY_VALUE_HEADS, HEAD_SIZE)[
        :, key_value_heads
    ]
    selected_values = value_row_matrix.reshape(resident_rows, KEY_VALUE_HEADS, HEAD_SIZE)[
        :, key_value_heads
    ]
    query_here, key_here, value_here = (
        lax.all_to_all(query_sel, "head", split_axis=1, concat_axis=0, tiled=True),
        lax.all_to_all(selected_keys, "head", split_axis=1, concat_axis=0, tiled=True),
        lax.all_to_all(selected_values, "head", split_axis=1, concat_axis=0, tiled=True),
    )
    seq_rows = query_here.shape[0]
    local_blocks = seq_rows // BLOCK_TOKENS
    my_heads = lax.dynamic_slice_in_dim(
        group_assign, lax.axis_index("head") * slot_count, slot_count
    )
    my_verticals = vertical_blocks[my_heads]
    my_offsets = slash_offsets[my_heads]
    key_before, value_before = passed_along((key_here, value_here), "seq", 1)
    seq_place = lax.axis_index("seq")
    block_local = my_verticals % local_blocks
    block_owner = my_verticals // local_blocks
    slot_column = jnp.arange(slot_count)[:, None]
    key_candidate = key_here.reshape(local_blocks, BLOCK_TOKENS, slot_count, HEAD_SIZE)[
        block_local, :, slot_column
    ]
    value_candidate = value_here.reshape(local_blocks, BLOCK_TOKENS, slot_count, HEAD_SIZE)[
        block_local, :, slot_column
    ]
    owned_here = (block_owner == seq_place)[:, :, None, None]
    summed_keys, summed_values = lax.psum(
        (
            jnp.where(owned_here, key_candidate.astype(jnp.float32), 0.0),
            jnp.where(owned_here, value_candidate.astype(jnp.float32), 0.0),
        ),
        "seq",
    )
    column_keys = summed_keys.astype(jnp.bfloat16)
    column_values = summed_values.astype(jnp.bfloat16)
    query_pos = seq_place * seq_rows + jnp.arange(seq_rows)
    query_block = query_pos // BLOCK_TOKENS
    window_pos = seq_place * seq_rows - seq_rows + jnp.arange(2 * seq_rows)
    window_block = jnp.floor_divide(window_pos, BLOCK_TOKENS)
    window_start = seq_place * local_blocks - local_blocks
    earlier = jnp.arange(NV)[:, None] < jnp.arange(NV)[None, :]
    scaling = 1.0 / math.sqrt(HEAD_SIZE)

    def attend_slot(head_slot):
        verticals = my_verticals[head_slot]
        offsets = my_offsets[head_slot]
        repeated = jnp.any((verticals[:, None] == verticals[None, :]) & earlier, axis=0)
        column_ok = (verticals < window_start) & jnp.logical_not(repeated)
        slash_hit = jnp.any(
            query_block[:, None, None] - window_block[None, :, None] == offsets[None, None, :],
            axis=2,
        )
        vertical_hit = jnp.any(window_block[:, None] == verticals[None, :], axis=1)
        window_ok = (
            (window_pos[None, :] >= 0)
            & (window_pos[None, :] <= query_pos[:, None])
            & (slash_hit | vertical_hit[None, :])
        )
        column_mask = jnp.broadcast_to(
            jnp.repeat(column_ok, BLOCK_TOKENS)[None, :], (seq_rows, NV * BLOCK_TOKENS)
        )
        allowed = jnp.concatenate([window_ok, column_mask], axis=1)
        all_keys = jnp.concatenate(
            [
                key_before[:, head_slot],
                key_here[:, head_slot],
                column_keys[head_slot].reshape(NV * BLOCK_TOKENS, HEAD_SIZE),
            ],
            axis=0,
        )
        all_values = jnp.concatenate(
            [
                value_before[:, head_slot],
                value_here[:, head_slot],
                column_values[head_slot].reshape(NV * BLOCK_TOKENS, HEAD_SIZE),
            ],
            axis=0,
        )
        scores = (
            lax.dot_general(
                query_here[:, head_slot],
                all_keys,
                (((1,), (1,)), ((), ())),
                preferred_element_type=jnp.float32,
            )
            * scaling
        )
        row_top = jnp.max(jnp.where(allowed, scores, -jnp.inf), axis=1, keepdims=True)
        weights = jnp.where(allowed, jnp.exp(scores - row_top), 0.0)
        row_total = jnp.sum(weights, axis=1, keepdims=True)
        blended = (
            jnp.dot(weights.astype(jnp.bfloat16), all_values, preferred_element_type=jnp.float32)
            / row_total
        )
        return blended.astype(jnp.bfloat16)

    attended_here = lax.map(attend_slot, jnp.arange(slot_count))
    arranged = jnp.transpose(attended_here, (1, 0, 2))
    returned = lax.all_to_all(arranged, "head", split_axis=0, concat_axis=1, tiled=True)
    return returned.reshape(returned.shape[0], QUERY_HEADS * HEAD_SIZE)


def solution(mesh):
    placed = (
        P(("seq", "head"), None),
        P(("seq", "head"), None),
        P(("seq", "head"), None),
        P(),
        P(),
        P(),
    )
    return jax.shard_map(
        per_device, mesh=mesh, in_specs=placed, out_specs=P(("seq", "head"), None), check_vma=False
    )
```

profile of v0, /device:TPU:27, one launch (start us, length us, event | category | flops | bytes accessed | tf_op | source)
XLA Modules:
  0.0 576.4 jit_solution(6912861411111241883)
XLA Ops:
  1.9 2.4 gather_fusion.3
  4.2 4.9 all-to-all-start.1
  9.2 2.4 gather_fusion.5
  11.6 27.2 %all-to-all-done.1 = bf16[160,64,128]{2,0,1:T(8,128)(2,1)} async-done(((bf16[160,64,128]{2,0,1:T(8,128)(2,1)}), bf16[160,64,128]{2,0,1:T(8,128)(2,1)}, u32[]{:S(2)}, u32[]{:S(2)}) %all-to-all-start.1) | async-done | bytes 2621472 | tf_op jit(solution)/shard_map/all_to_all | solution.py:38
  38.8 4.9 all-to-all-start.2
  45.7 4.1 gather_fusion.2
  49.8 22.8 %all-to-all-done.2 = bf16[160,64,128]{2,0,1:T(8,128)(2,1)} async-done(((bf16[160,64,128]{2,0,1:T(8,128)(2,1)}), bf16[160,64,128]{2,0,1:T(8,128)(2,1)}, u32[]{:S(2)}, u32[]{:S(2)}) %all-to-all-start.2) | async-done | bytes 2621472 | tf_op jit(solution)/shard_map/all_to_all | solution.py:39
  72.6 5.8 %all-to-all-start = ((bf16[160,64,128]{2,0,1:T(8,128)(2,1)}), bf16[160,64,128]{2,0,1:T(8,128)(2,1)}, u32[]{:S(2)}, u32[]{:S(2)}) async-start(bf16[160,64,128]{2,0,1:T(8,128)(2,1)} %bitcast), calls=%async_computation | async-start | bytes 5242880 | tf_op jit(solution)/shard_map/all_to_all | solution.py:37
  80.2 2.8 copy.76
  84.2 2.2 copy.88
  86.5 4.3 copy.83
  92.0 4.0 copy.90
  96.0 2.2 copy.80
  98.2 3.9 copy.85
  102.2 3.9 gather_fusion.4
  106.1 3.9 gather_fusion.6
  110.0 6.8 %convert_select_fusion = (f32[16,4,128,128]{3,2,1,0:T(8,128)}, f32[16,4,128,128]{3,2,1,0:T(8,128)}) fusion(bf16[16,4,128,128]{3,2,1,0:T(8,128)(2,1)} %bitcast.123, pred[16,4]{1,0:T(8,128)(4,1)S(1)} %fusion.56, bf16[16,4,128,128]{3,2,1,0:T(8,128)(2,1)} %bitcast.122), kind=kLoop, calls=%fused_computation.79 | loop fusion | flops 4194304 | bytes 12582976 | tf_op jit(solution)/shard_map/jit(_where)/select_n | solution.py:63
  116.8 2.8 copy.73
  119.6 2.1 copy.86
  121.7 180.0 %all-reduce.2 = (bf16[16,4,128,128]{3,2,1,0:T(8,128)(2,1)}, bf16[16,4,128,128]{3,2,1,0:T(8,128)(2,1)}) all-reduce(f32[16,4,128,128]{3,2,1,0:T(8,128)} %get-tuple-element.287, f32[16,4,128,128]{3,2,1,0:T(8,128)} %get-tuple-element.286), channel_id=1, replica_groups=mesh['seq'=8,'head'=4] {'seq'}, use_global_device_ids=true, to_apply=%region_0.1 | all-reduce | flops 2097152 | bytes 12582912 | tf_op jit(solution)/shard_map/psum | solution.py:60
  301.7 3.9 copy.87
  305.7 3.9 copy.89
  309.6 228.7 %while.12 = (s32[]{:T(128)}, bf16[16,640,128]{2,1,0:T(8,128)(2,1)}, s32[16]{0:T(128)S(1)}, s32[16,3]{1,0:T(8,128)S(1)}, s32[16,4]{1,0:T(8,128)S(1)}, /*index=5*/...) while((s32[]{:T(128)}, bf16[16,640,128]{2,1,0:T(8,128)(2,1)}, ...), condition=%wide.region_8.9_spmd.clone.clone, body=%wide.region_2.8_spmd.clone.clone.sunk | while | flops 614408256 | bytes 28374412 | solution.py:130
  312.1 2.4 compare_reduce_fusion.4
  317.7 2.0 select_reduce_fusion.2
  326.4 2.4 compare_reduce_fusion.4
  340.7 2.4 compare_reduce_fusion.4
  346.3 2.0 select_reduce_fusion.2
  355.0 2.4 compare_reduce_fusion.4
  369.3 2.4 compare_reduce_fusion.4
  374.9 2.0 select_reduce_fusion.2
  383.6 2.4 compare_reduce_fusion.4
  397.9 2.4 compare_reduce_fusion.4
  403.5 2.0 select_reduce_fusion.2
  412.2 2.4 compare_reduce_fusion.4
  426.5 2.4 compare_reduce_fusion.4
  432.1 2.0 select_reduce_fusion.2
  440.8 2.4 compare_reduce_fusion.4
  455.1 2.4 compare_reduce_fusion.4
  469.4 2.4 compare_reduce_fusion.4
  483.7 2.4 compare_reduce_fusion.4
  498.0 2.4 compare_reduce_fusion.4
  512.3 2.4 compare_reduce_fusion.4
  517.9 2.0 select_reduce_fusion.2
  526.6 2.4 compare_reduce_fusion.4
  538.3 3.4 copy.108
  541.8 29.9 %all_to_all.69 = bf16[640,16,128]{2,1,0:T(8,128)(2,1)S(1)} all-to-all(bf16[640,16,128]{2,1,0:T(8,128)(2,1)S(1)} %bitcast.119), channel_id=1, replica_groups=mesh['seq'=8,'head'=4] {'head'}, dimensions={0} | all-to-all | bytes 5242880 | tf_op jit(solution)/shard_map/all_to_all | solution.py:132
  572.5 3.9 copy.107
  (335 shorter events, 161.1 us)
Async XLA Ops:
  0.0 43.7 %copy-start = (bf16[160,8192]{1,0:T(8,128)(2,1)S(1)}, bf16[160,8192]{1,0:T(8,128)(2,1)}, u32[]{:S(2)}) copy-start(bf16[160,8192]{1,0:T(8,128)(2,1)} %param.8) | copy-start | bytes 7864324
  4.2 4.9 copy-start.2
  4.2 34.6 %all-to-all-start.1 = ((bf16[160,64,128]{2,0,1:T(8,128)(2,1)}), bf16[160,64,128]{2,0,1:T(8,128)(2,1)}, u32[]{:S(2)}, u32[]{:S(2)}) async-start(bf16[160,64,128]{2,0,1:T(8,128)(2,1)} %bitcast.117), calls=%async_computation.1 | async-start | bytes 5242880 | tf_op jit(solution)/shard_map/all_to_all | solution.py:38
  38.8 33.8 %all-to-all-start.2 = ((bf16[160,64,128]{2,0,1:T(8,128)(2,1)}), bf16[160,64,128]{2,0,1:T(8,128)(2,1)}, u32[]{:S(2)}, u32[]{:S(2)}) async-start(bf16[160,64,128]{2,0,1:T(8,128)(2,1)} %bitcast.116), calls=%async_computation.2 | async-start | bytes 5242880 | tf_op jit(solution)/shard_map/all_to_all | solution.py:39
  72.6 5.9 %copy-start.3 = (s32[64,4]{0,1:T(4,128)S(1)}, s32[64,4]{0,1:T(4,128)}, u32[]{:S(2)}) copy-start(s32[64,4]{0,1:T(4,128)} %param.12) | copy-start | bytes 3076
  72.6 6.0 %copy-start.5 = (s32[64]{0:T(128)S(1)}, s32[64]{0:T(128)}, u32[]{:S(2)}) copy-start(s32[64]{0:T(128)} %param.11) | copy-start | bytes 772
  72.6 6.9 %copy-start.4 = (s32[64,3]{0,1:T(4,128)S(1)}, s32[64,3]{0,1:T(4,128)}, u32[]{:S(2)}) copy-start(s32[64,3]{0,1:T(4,128)} %param.13) | copy-start | bytes 2308
  72.6 44.2 %all-to-all-start = ((bf16[160,64,128]{2,0,1:T(8,128)(2,1)}), bf16[160,64,128]{2,0,1:T(8,128)(2,1)}, u32[]{:S(2)}, u32[]{:S(2)}) async-start(bf16[160,64,128]{2,0,1:T(8,128)(2,1)} %bitcast), calls=%async_computation | async-start | bytes 5242880 | tf_op jit(solution)/shard_map/all_to_all | solution.py:37
  82.9 218.8 %collective-permute-start = (bf16[640,16,128]{2,1,0:T(8,128)(2,1)S(1)}, bf16[640,16,128]{2,1,0:T(8,128)(2,1)}, u32[]{:S(2)}, u32[]{:S(2)}) collective-permute-start(bf16[640,16,128]{2,1,0:T(8,128)(2,1)S(1)} %bitcast.113), channel_id=1, source_target_pairs={{0,4},{4,8},{8,12},{12,16},{16,20},{20,24},{24,28},{1,5},{5,9},{9,... | collective-permute-start | bytes 7864328 | tf_op jit(solution)/shard_map/ppermute | solution.py:18
  90.8 214.9 %collective-permute-start.1 = (bf16[640,16,128]{2,1,0:T(8,128)(2,1)}, bf16[640,16,128]{2,1,0:T(8,128)(2,1)}, u32[]{:S(2)}, u32[]{:S(2)}) collective-permute-start(bf16[640,16,128]{2,1,0:T(8,128)(2,1)} %bitcast.19), channel_id=1, source_target_pairs={{0,4},{4,8},{8,12},{12,16},{16,20},{20,24},{24,28},{1,5},{5,9},{9,... | collective-permute-start | bytes 7864328 | tf_op jit(solution)/shard_map/ppermute | solution.py:18
  572.5 3.9 copy-start.1
where the time goes:
time: 587 us; the launch traced here: 576 us
  blocking collectives  210 us (36%)
  local copies, waits for them, and re-layouts  121 us (21%)
  other arithmetic  89.1 us (15%)
  matrix products  61.2 us (10%)
  waiting for transfers between devices  50 us (9%)
  loops' own time  27.2 us (5%)
  starting transfers between devices  18.2 us (3%)
    psum x1, blocking collectives, per_device(): lax.psum((jnp.where(owned_here, key_candidate.astype(jnp.float32), 0.0),...  180 us
    reduce_or x16, other arithmetic, attend_slot(): jnp.any(query_block[:, None, None] - window_block[None, :, None] == offse...  37.7 us
    dot_general x16, matrix products, attend_slot(): lax.dot_general(query_here[:, head_slot], all_keys, (((1,), (1,)), ((), (...  31.4 us
    all_to_all x1, blocking collectives, per_device(): lax.all_to_all(arranged, 'head', split_axis=0, concat_axis=1, tiled=True)  29.9 us
    dot_general x16, matrix products, attend_slot(): jnp.dot(weights.astype(jnp.bfloat16), all_values, preferred_element_type=...  29.8 us
    all_to_all x1, waiting for transfers between devices, per_device(): lax.all_to_all(selected_keys, 'head', split_axis=1, concat_axis=0, tiled=...  27.2 us
    another operation x1, loops' own time, per_device(): attended_here = lax.map(attend_slot, jnp.arange(slot_count))  27.2 us
    all_to_all x1, waiting for transfers between devices, per_device(): lax.all_to_all(selected_values, 'head', split_axis=1, concat_axis=0, tile...  22.8 us
  transfers between devices with their start and end apart: 5, of which 2 were waited for; matrix products, arithmetic and copies ran while one was open for 9% of the time, Pallas kernels for 0%

commit v1 on v0

v1 whole, which is shorter than its diff:
```python
import functools
import math

import jax
import jax.numpy as jnp
from jax import lax
from jax.experimental import pallas as pl
from jax.experimental.pallas import tpu as pltpu
from jax.sharding import PartitionSpec as P

QUERY_HEADS = 64
KEY_VALUE_HEADS = 8
HEAD_SIZE = 128
BLOCK_TOKENS = 128
SHARING = QUERY_HEADS // KEY_VALUE_HEADS
VMEM_BYTES = 56 * 1024 * 1024


def block_attention(query, keys_ref, values_ref, block, offsets, verticals):
    factor = math.log2(math.e) / math.sqrt(HEAD_SIZE)
    blocks, valid = [], []
    for offset in offsets:
        blocks.append(jnp.maximum(block - offset, 0))
        valid.append(block - offset >= 0)
    for n, vertical in enumerate(verticals):
        ok = vertical <= block
        for offset in offsets:
            ok = ok & (block - vertical != offset)
        for other in verticals[:n]:
            ok = ok & (vertical != other)
        blocks.append(jnp.minimum(vertical, block))
        valid.append(ok)
    places = [pl.ds(pl.multiple_of(b * BLOCK_TOKENS, BLOCK_TOKENS), BLOCK_TOKENS) for b in blocks]
    keys = jnp.concatenate([keys_ref[place, :] for place in places], axis=0)
    scores = lax.dot_general(
        query, keys, (((1,), (1,)), ((), ())), preferred_element_type=jnp.float32
    )
    parts = []
    for n in range(len(places)):
        part = scores[:, n * BLOCK_TOKENS : (n + 1) * BLOCK_TOKENS]
        if n == 0:
            rows = lax.broadcasted_iota(jnp.int32, part.shape, 0)
            columns = lax.broadcasted_iota(jnp.int32, part.shape, 1)
            part = jnp.where(columns <= rows, part, -jnp.inf)
        else:
            part = part + jnp.where(valid[n], 0.0, -jnp.inf)
        parts.append(part)
    top = functools.reduce(jnp.maximum, parts)
    row_top = jnp.max(top, axis=1, keepdims=True)
    weights = [jnp.exp2((part - row_top) * factor) for part in parts]
    row_total = jnp.sum(functools.reduce(jnp.add, weights), axis=1, keepdims=True)
    rounded = jnp.concatenate([w.astype(jnp.bfloat16) for w in weights], axis=1)
    values = jnp.concatenate([values_ref[place, :] for place in places], axis=0)
    blended = jnp.dot(rounded, values, preferred_element_type=jnp.float32)
    return (blended / row_total).astype(jnp.bfloat16)


def attention_kernel(share, nv, ns, place_ref, vert_ref, slash_ref, q_ref, k_ref, v_ref, o_ref):
    local_blocks = q_ref.shape[0] // BLOCK_TOKENS
    head = place_ref[1] + pl.program_id(0) * share + pl.program_id(1)
    offsets = [slash_ref[head * ns + n] for n in range(ns)]
    verticals = [vert_ref[head * nv + n] for n in range(nv)]
    for n in range(local_blocks):
        rows = pl.ds(n * BLOCK_TOKENS, BLOCK_TOKENS)
        block = place_ref[0] * local_blocks + n
        o_ref[rows, :] = block_attention(
            q_ref[rows, :], k_ref, v_ref, block, offsets, verticals
        )


def attend(query, keys_values, place, vertical_blocks, slash_offsets, kv_count):
    rows, width = query.shape
    heads = width // HEAD_SIZE
    share = heads // kv_count
    tokens = keys_values.shape[0]
    nv, ns = vertical_blocks.shape[1], slash_offsets.shape[1]
    pairs = heads * (rows // BLOCK_TOKENS) * (nv + ns)
    return pl.pallas_call(
        functools.partial(attention_kernel, share, nv, ns),
        grid_spec=pltpu.PrefetchScalarGridSpec(
            num_scalar_prefetch=3,
            grid=(kv_count, share),
            in_specs=[
                pl.BlockSpec((rows, HEAD_SIZE), lambda i, j, *_: (0, i * share + j)),
                pl.BlockSpec((tokens, HEAD_SIZE), lambda i, j, *_: (0, i)),
                pl.BlockSpec((tokens, HEAD_SIZE), lambda i, j, *_: (0, kv_count + i)),
            ],
            out_specs=pl.BlockSpec((rows, HEAD_SIZE), lambda i, j, *_: (0, i * share + j)),
        ),
        out_shape=jax.ShapeDtypeStruct(query.shape, query.dtype),
        compiler_params=pltpu.CompilerParams(vmem_limit_bytes=VMEM_BYTES),
        cost_estimate=pl.CostEstimate(
            flops=pairs * 4 * BLOCK_TOKENS * BLOCK_TOKENS * HEAD_SIZE,
            bytes_accessed=2 * query.nbytes + keys_values.nbytes,
            transcendentals=pairs * BLOCK_TOKENS * BLOCK_TOKENS,
        ),
    )(place, vertical_blocks.reshape(-1), slash_offsets.reshape(-1), query, keys_values, keys_values)


def reorder_kernel(per_step, assign_ref, x_ref, o_ref):
    step = pl.program_id(0)
    for n in range(per_step):
        source = assign_ref[step * per_step + n]
        column = pl.ds(pl.multiple_of(source * HEAD_SIZE, HEAD_SIZE), HEAD_SIZE)
        o_ref[:, n * HEAD_SIZE : (n + 1) * HEAD_SIZE] = x_ref[:, column]


def reorder(x, assign):
    per_step = 8
    rows, width = x.shape
    return pl.pallas_call(
        functools.partial(reorder_kernel, per_step),
        grid_spec=pltpu.PrefetchScalarGridSpec(
            num_scalar_prefetch=1,
            grid=(width // HEAD_SIZE // per_step,),
            in_specs=[pl.BlockSpec((rows, width), lambda i, *_: (0, 0))],
            out_specs=pl.BlockSpec((rows, per_step * HEAD_SIZE), lambda i, *_: (0, i)),
        ),
        out_shape=jax.ShapeDtypeStruct(x.shape, x.dtype),
        compiler_params=pltpu.CompilerParams(vmem_limit_bytes=VMEM_BYTES),
        cost_estimate=pl.CostEstimate(flops=0, bytes_accessed=2 * x.nbytes, transcendentals=0),
    )(assign, x)


def per_device(
    query_rows, rotated_key_rows, value_row_matrix, group_assign, vertical_blocks, slash_offsets
):
    groups = lax.axis_size("head")
    heads = QUERY_HEADS // groups
    kv_count = max(1, heads // SHARING)
    kv_width = kv_count * HEAD_SIZE
    pieces = []
    for g in range(groups):
        first = g * heads // SHARING * HEAD_SIZE
        pieces.append(rotated_key_rows[:, first : first + kv_width])
        pieces.append(value_row_matrix[:, first : first + kv_width])
    keys_values = jnp.concatenate(pieces, axis=1)
    keys_values = lax.all_to_all(keys_values, "head", split_axis=1, concat_axis=0, tiled=True)
    query_here = lax.all_to_all(query_rows, "head", split_axis=1, concat_axis=0, tiled=True)
    all_keys_values = lax.all_gather(keys_values, "seq", axis=0, tiled=True)
    place = jnp.stack([lax.axis_index("seq"), lax.axis_index("head") * heads]).astype(jnp.int32)
    attended = attend(
        query_here, all_keys_values, place, vertical_blocks, slash_offsets, kv_count
    )
    returned = lax.all_to_all(attended, "head", split_axis=0, concat_axis=1, tiled=True)
    return reorder(returned, group_assign)


def solution(mesh):
    placed = (
        P(("seq", "head"), None),
        P(("seq", "head"), None),
        P(("seq", "head"), None),
        P(),
        P(),
        P(),
    )
    return jax.shard_map(
        per_device, mesh=mesh, in_specs=placed, out_specs=P(("seq", "head"), None), check_vma=False
    )
```

time: 587 us -> 170 us (0.29)
  the two profiles are of different devices: /device:TPU:27 before, /device:TPU:0 now
where the time goes in v1:
time: 170 us; the launch traced here: 169 us
  blocking collectives  50.3 us (30%)
  waiting for transfers between devices  48.2 us (28%)
  Pallas kernels  40 us (24%)
  between operations  13.4 us (8%)
  local copies, waits for them, and re-layouts  12.5 us (7%)
  starting transfers between devices  3.79 us (2%)
    all_to_all x1, blocking collectives, per_device(): lax.all_to_all(attended, 'head', split_axis=0, concat_axis=1, tiled=True)  35.3 us
    pallas_call x1, Pallas kernels, attend(): pl.pallas_call(functools.partial(attention_kernel, share, nv, ns), grid_s...  34.2 us
    all_to_all x1, waiting for transfers between devices, per_device(): lax.all_to_all(query_rows, 'head', split_axis=1, concat_axis=0, tiled=True)  26.9 us
    all_gather x1, waiting for transfers between devices, per_device(): all_keys_values = lax.all_gather(keys_values, 'seq', axis=0, tiled=True)  21.2 us
    all_to_all x1, blocking collectives, per_device(): lax.all_to_all(keys_values, 'head', split_axis=1, concat_axis=0, tiled=True)  15 us
    unnamed x17, local copies, waits for them, and re-layouts  6.62 us
    pallas_call x1, Pallas kernels, reorder(): pl.pallas_call(functools.partial(reorder_kernel, per_step), grid_spec=plt...  5.77 us
    all_to_all x1, starting transfers between devices, per_device(): lax.all_to_all(query_rows, 'head', split_axis=1, concat_axis=0, tiled=True)  3.79 us
  transfers between devices with their start and end apart: 2, of which 2 were waited for; matrix products, arithmetic and copies ran while one was open for 2% of the time, Pallas kernels for 0%

profile of v1, /device:TPU:0, one launch (start us, length us, event | category | flops | bytes accessed | tf_op | source)
XLA Modules:
  0.0 168.8 jit_solution(5614149220791493251)
XLA Ops:
  6.5 0.0 copy-start
  6.5 0.0 all-gather.2.cloned.1.call-start
  6.5 1.0 slice_dynamic-update-slice_fusion.7
  7.6 0.9 slice_dynamic-update-slice_fusion.6
  8.5 0.9 slice_dynamic-update-slice_fusion.5
  9.4 0.9 slice_dynamic-update-slice_fusion.4
  10.3 0.9 slice_dynamic-update-slice_fusion.3
  11.2 0.9 slice_dynamic-update-slice_fusion.2
  12.1 0.9 slice_dynamic-update-slice_fusion.1
  13.0 0.9 slice_dynamic-update-slice_fusion
  13.9 0.1 copy.26
  13.9 15.0 %all_to_all.57 = bf16[160,4,512]{2,0,1:T(8,128)(2,1)} all-to-all(bf16[160,4,512]{2,0,1:T(8,128)(2,1)S(1)} %bitcast.26), channel_id=1, replica_groups=mesh['seq'=8,'head'=4] {'head'}, dimensions={1} | all-to-all | bytes 1310720 | tf_op jit(solution)/shard_map/all_to_all | solution.py:138
  28.9 0.0 all-gather.2.cloned.1.call-update
  28.9 0.0 copy-done
  28.9 1.7 copy.25
  30.6 0.0 copy-start.2
  30.6 0.0 copy-start.3
  30.6 3.8 %all-to-all-start = ((bf16[160,4,2048]{2,0,1:T(8,128)(2,1)}), bf16[160,4,2048]{2,0,1:T(8,128)(2,1)S(1)}, u32[]{:S(2)}, u32[]{:S(2)}) async-start(bf16[160,4,2048]{2,0,1:T(8,128)(2,1)} %bitcast.18), calls=%async_computation | async-start | bytes 5242880 | tf_op jit(solution)/shard_map/all_to_all | solution.py:139
  34.4 0.0 copy-done.2
  34.4 0.1 copy.15
  34.5 0.7 reshape.15.vert_ref
  35.2 0.0 copy-done.3
  35.2 0.1 copy.16
  35.3 0.7 reshape.16.slash_ref
  36.0 0.6 pad_add_fusion.place_ref
  36.7 26.9 %all-to-all-done = bf16[160,4,2048]{2,0,1:T(8,128)(2,1)S(1)} async-done(((bf16[160,4,2048]{2,0,1:T(8,128)(2,1)}), bf16[160,4,2048]{2,0,1:T(8,128)(2,1)S(1)}, u32[]{:S(2)}, u32[]{:S(2)}) %all-to-all-start) | async-done | bytes 2621472 | tf_op jit(solution)/shard_map/all_to_all | solution.py:139
  63.6 0.0 copy-start.1
  63.6 21.2 %all-gather.2.cloned.1.call-done.k_ref.v_ref = bf16[5120,512]{1,0:T(8,128)(2,1)} async-done(((bf16[640,512]{1,0:T(8,128)(2,1)}), bf16[5120,512]{1,0:T(8,128)(2,1)}) %all-gather.2.cloned.1.call-update) | async-done | bytes 5242896 | tf_op jit(solution)/shard_map/all_gather | solution.py:140
  84.9 0.0 copy-done.1
  84.9 34.2 %shard_map.64 = bf16[640,2048]{1,0:T(8,128)(2,1)} custom-call(s32[2]{0:T(128)} %pad_add_fusion.place_ref, s32[256]{0:T(256)} %reshape.15.vert_ref, s32[192]{0:T(256)} %reshape.16.slash_ref, bf16[640,2048]{1,0:T(8,128)(2,1)} %bitcast.23, bf16[5120,512]{1,0:T(8,128)(2,1)} %all-gather.2.cloned.1.call-done.k_ref.v_ref, ...), custom_call_target="tpu_custom_call" | custom-call | flops 4697620480 | bytes 10485760 | tf_op jit(solution)/shard_map/pallas_call | solution.py:78
  119.1 35.3 %all_to_all.58 = bf16[4,160,2048]{2,1,0:T(8,128)(2,1)S(1)} all-to-all(bf16[4,160,2048]{2,1,0:T(8,128)(2,1)} %bitcast.24), channel_id=1, replica_groups=mesh['seq'=8,'head'=4] {'head'}, dimensions={0} | all-to-all | bytes 5242880 | tf_op jit(solution)/shard_map/all_to_all | solution.py:145
  154.4 1.8 %copy.22 = bf16[4,20,8,2048]{3,2,0,1:T(8,128)(2,1)} copy(bf16[4,20,8,2048]{3,2,1,0:T(8,128)(2,1)S(1)} %bitcast.20) | data formatting | bytes 5242880 | tf_op jit(solution)/shard_map/all_to_all | solution.py:145
  156.2 5.8 %shard_map.65 = bf16[160,8192]{1,0:T(8,128)(2,1)} custom-call(s32[64]{0:T(128)} %assign_ref.1, bf16[160,8192]{1,0:T(8,128)(2,1)} %bitcast.21), custom_call_target="tpu_custom_call" | custom-call | bytes 5242880 | tf_op jit(solution)/shard_map/pallas_call | solution.py:111
Async XLA Ops:
  6.5 22.4 %copy-start = (bf16[160,8192]{1,0:T(8,128)(2,1)S(1)}, bf16[160,8192]{1,0:T(8,128)(2,1)}, u32[]{:S(2)}) copy-start(bf16[160,8192]{1,0:T(8,128)(2,1)} %param.6) | copy-start | bytes 7864324
  6.5 78.3 %all-gather.2.cloned.1.call-start = ((), (), s32[]{:S(2)}) async-start(), calls=%async_computation.3 | async-start | bytes 5898240 | tf_op jit(solution)/shard_map/all_gather | solution.py:140
  30.6 3.8 %copy-start.2 = (s32[64,4]{0,1:T(4,128)S(1)}, s32[64,4]{0,1:T(4,128)}, u32[]{:S(2)}) copy-start(s32[64,4]{0,1:T(4,128)} %param.10) | copy-start | bytes 3076
  30.6 4.6 %copy-start.3 = (s32[64,3]{0,1:T(4,128)S(1)}, s32[64,3]{0,1:T(4,128)}, u32[]{:S(2)}) copy-start(s32[64,3]{0,1:T(4,128)} %param.11) | copy-start | bytes 2308
  30.6 33.0 %all-to-all-start = ((bf16[160,4,2048]{2,0,1:T(8,128)(2,1)}), bf16[160,4,2048]{2,0,1:T(8,128)(2,1)S(1)}, u32[]{:S(2)}, u32[]{:S(2)}) async-start(bf16[160,4,2048]{2,0,1:T(8,128)(2,1)} %bitcast.18), calls=%async_computation | async-start | bytes 5242880 | tf_op jit(solution)/shard_map/all_to_all | solution.py:139
  63.6 21.3 %copy-start.1 = (bf16[160,4,2048]{2,0,1:T(8,128)(2,1)}, bf16[160,4,2048]{2,0,1:T(8,128)(2,1)S(1)}, u32[]{:S(2)}) copy-start(bf16[160,4,2048]{2,0,1:T(8,128)(2,1)S(1)} %all-to-all-done) | copy-start | bytes 7864324
Sparse Core Ops, SparseCore 0:
  29.1 55.7 all-gather.1

commit v2 on v1

v2 whole, which is shorter than its diff:
```python
import functools
import math

import jax
import jax.numpy as jnp
from jax import lax
from jax.experimental import pallas as pl
from jax.experimental.pallas import tpu as pltpu
from jax.sharding import PartitionSpec as P

QUERY_HEADS = 64
KEY_VALUE_HEADS = 8
HEAD_SIZE = 128
BLOCK_TOKENS = 128
SHARING = QUERY_HEADS // KEY_VALUE_HEADS
VMEM_BYTES = 56 * 1024 * 1024


def block_attention(query, keys_values, key_column, value_column, block, offsets, verticals):
    factor = math.log2(math.e) / math.sqrt(HEAD_SIZE)
    blocks, valid = [], []
    for offset in offsets:
        blocks.append(jnp.maximum(block - offset, 0))
        valid.append(block - offset >= 0)
    for n, vertical in enumerate(verticals):
        ok = vertical <= block
        for offset in offsets:
            ok = ok & (block - vertical != offset)
        for other in verticals[:n]:
            ok = ok & (vertical != other)
        blocks.append(jnp.minimum(vertical, block))
        valid.append(ok)
    per_block = BLOCK_TOKENS // keys_values.shape[1]
    shape = (BLOCK_TOKENS, HEAD_SIZE)

    def gathered(column):
        return jnp.concatenate(
            [
                keys_values[pl.ds(b * per_block, per_block), :, column : column + HEAD_SIZE].reshape(shape)
                for b in blocks
            ],
            axis=0,
        )

    keys = gathered(key_column)
    scores = lax.dot_general(
        query, keys, (((1,), (1,)), ((), ())), preferred_element_type=jnp.float32
    )
    parts = []
    for n in range(len(blocks)):
        part = scores[:, n * BLOCK_TOKENS : (n + 1) * BLOCK_TOKENS]
        if n == 0:
            rows = lax.broadcasted_iota(jnp.int32, part.shape, 0)
            columns = lax.broadcasted_iota(jnp.int32, part.shape, 1)
            part = jnp.where(columns <= rows, part, -jnp.inf)
        else:
            part = part + jnp.where(valid[n], 0.0, -jnp.inf)
        parts.append(part)
    top = functools.reduce(jnp.maximum, parts)
    row_top = jnp.max(top, axis=1, keepdims=True)
    weights = [jnp.exp2((part - row_top) * factor) for part in parts]
    row_total = jnp.sum(functools.reduce(jnp.add, weights), axis=1, keepdims=True)
    rounded = jnp.concatenate([w.astype(jnp.bfloat16) for w in weights], axis=1)
    values = gathered(value_column)
    blended = jnp.dot(rounded, values, preferred_element_type=jnp.float32)
    return (blended / row_total).astype(jnp.bfloat16)


MESH = pl.DeviceIdType.MESH


def columns_of(start, count):
    return pl.ds(pl.multiple_of(start * count, HEAD_SIZE), count)


def units_of(start, count):
    return pl.ds(start * count, count)


def fused_kernel(
    nv, ns, assign_ref, vert_ref, slash_ref, query_ref, key_ref, value_ref, out_ref,
    queries, keys_values, attended, received,
    kv_send, kv_recv, q_send, q_recv, o_send, o_recv, own_sem, mine_sem,
    up_send, up_recv, pair_send, pair_recv,
):
    groups, seq_count = lax.axis_size("head"), lax.axis_size("seq")
    group, seq = lax.axis_index("head"), lax.axis_index("seq")
    chips = seq_count // 2
    core = lax.rem(seq, 2)
    pair = seq + 1 - 2 * core
    resident, unit = query_ref.shape[:2]
    heads = QUERY_HEADS // groups
    width = heads * HEAD_SIZE
    kv_width = keys_values.shape[2] // 2
    kv_count = kv_width // HEAD_SIZE
    share = heads // kv_count
    seq_rows = resident * groups
    per_block = BLOCK_TOKENS // unit
    local_blocks = seq_rows // per_block
    above, below = seq + 2 < seq_count, seq >= 2

    barrier = pltpu.get_barrier_semaphore()
    for d in range(1, groups):
        pl.semaphore_signal(
            barrier, inc=1, device_id={"head": lax.rem(group + d, groups)}, device_id_type=MESH
        )
    pl.semaphore_signal(barrier, inc=1, device_id={"seq": pair}, device_id_type=MESH)

    @pl.when(above)
    def _():
        pl.semaphore_signal(barrier, inc=1, device_id={"seq": seq + 2}, device_id_type=MESH)

    @pl.when(below)
    def _():
        pl.semaphore_signal(barrier, inc=1, device_id={"seq": seq - 2}, device_id_type=MESH)

    pl.semaphore_wait(barrier, groups + above.astype(jnp.int32) + below.astype(jnp.int32))

    def kv_columns(g):
        first = lax.div(g * heads, SHARING) * HEAD_SIZE
        return pl.ds(pl.multiple_of(first, HEAD_SIZE), kv_width)

    def kv_rows(g):
        return pl.ds(seq * seq_rows + g * resident, resident)

    def kv_copy(d, part, target, owner):
        source = (key_ref, value_ref)[part]
        return pltpu.make_async_remote_copy(
            src_ref=source.at[:, :, kv_columns(target)],
            dst_ref=keys_values.at[kv_rows(owner), :, pl.ds(part * kv_width, kv_width)],
            send_sem=kv_send.at[d, part],
            recv_sem=kv_recv.at[d, part],
            device_id={"head": target},
            device_id_type=MESH,
        )

    def q_copy(d, target, owner):
        return pltpu.make_async_remote_copy(
            src_ref=query_ref.at[:, :, columns_of(target, width)],
            dst_ref=queries.at[units_of(owner, resident)],
            send_sem=q_send.at[d],
            recv_sem=q_recv.at[d],
            device_id={"head": target},
            device_id_type=MESH,
        )

    def o_copy(d, h, target, owner):
        return pltpu.make_async_remote_copy(
            src_ref=attended.at[h, units_of(target, resident)],
            dst_ref=received.at[owner * heads + h],
            send_sem=o_send.at[d, h],
            recv_sem=o_recv.at[d, h],
            device_id={"head": target},
            device_id_type=MESH,
        )

    def mine_copy(h):
        return pltpu.make_async_copy(
            attended.at[h, units_of(group, resident)],
            received.at[group * heads + h],
            mine_sem.at[h],
        )

    def block_rows(b):
        return keys_values.at[units_of(b, seq_rows)]

    def up_copy(k, block, target, sem):
        return pltpu.make_async_remote_copy(
            src_ref=block_rows(block),
            dst_ref=block_rows(block),
            send_sem=up_send.at[k],
            recv_sem=up_recv.at[sem],
            device_id={"seq": target},
            device_id_type=MESH,
        )

    def pair_copy(k, block):
        return pltpu.make_async_remote_copy(
            src_ref=block_rows(block),
            dst_ref=block_rows(block),
            send_sem=pair_send.at[k],
            recv_sem=pair_recv.at[k],
            device_id={"seq": pair},
            device_id_type=MESH,
        )

    def later(d):
        return lax.rem(group + d, groups)

    def before(d):
        return lax.rem(group + groups - d, groups)

    for d in range(1, groups):
        for part in range(2):
            kv_copy(d, part, later(d), group).start()
    own = [
        pltpu.make_async_copy(
            source.at[:, :, kv_columns(group)],
            keys_values.at[kv_rows(group), :, pl.ds(part * kv_width, kv_width)],
            own_sem.at[part],
        )
        for part, source in enumerate((key_ref, value_ref))
    ]
    own.append(
        pltpu.make_async_copy(
            query_ref.at[:, :, columns_of(group, width)],
            queries.at[units_of(group, resident)],
            own_sem.at[2],
        )
    )
    for copy in own:
        copy.start()
    for d in range(1, groups):
        q_copy(d, later(d), group).start()
    own[0].wait()
    own[1].wait()
    for d in range(1, groups):
        for part in range(2):
            kv_copy(d, part, group, before(d)).wait_recv()

    for k in range(chips):
        block = seq - 2 * k
        held = block >= 0

        if k:

            @pl.when(held)
            def _():
                up_copy(k, block, seq, k).wait_recv()

        @pl.when(held & above)
        def _():
            up_copy(k, block, seq + 2, k + 1).start()

        @pl.when((held & (core == 0)) if k == 0 else held)
        def _():
            pair_copy(k, block).start()

    for k in range(chips):
        arrives = (core == 1) if k == 0 else pair - 2 * k >= 0

        @pl.when(arrives)
        def _():
            pair_copy(k, pair - 2 * k).wait_recv()

    own[2].wait()
    for d in range(1, groups):
        q_copy(d, group, before(d)).wait_recv()

    for kv in range(kv_count):
        key_column = kv * HEAD_SIZE

        def one_head(j, carry):
            h = kv * share + j
            head = group * heads + h
            offsets = [slash_ref[head * ns + n] for n in range(ns)]
            verticals = [vert_ref[head * nv + n] for n in range(nv)]
            column = columns_of(h, HEAD_SIZE)
            for n in range(local_blocks):
                part = pl.ds(n * per_block, per_block)
                blended = block_attention(
                    queries[part, :, column].reshape(BLOCK_TOKENS, HEAD_SIZE),
                    keys_values,
                    key_column,
                    kv_width + key_column,
                    seq * local_blocks + n,
                    offsets,
                    verticals,
                )
                attended[h, part] = blended.reshape(per_block, unit, HEAD_SIZE)
            for d in range(1, groups):
                o_copy(d, h, later(d), group).start()
            mine_copy(h).start()
            return carry

        lax.fori_loop(0, share, one_head, 0)

    def land(h, carry):
        mine_copy(h).wait()
        for d in range(1, groups):
            o_copy(d, h, group, before(d)).wait_recv()
        return carry

    lax.fori_loop(0, heads, land, 0)

    for k in range(QUERY_HEADS):
        out_ref[:, :, k * HEAD_SIZE : (k + 1) * HEAD_SIZE] = received[assign_ref[k]]

    def sent(h, carry):
        for d in range(1, groups):
            o_copy(d, h, later(d), group).wait_send()
        return carry

    lax.fori_loop(0, heads, sent, 0)
    for d in range(1, groups):
        q_copy(d, later(d), group).wait_send()
        for part in range(2):
            kv_copy(d, part, later(d), group).wait_send()
    for k in range(chips):
        block = seq - 2 * k
        held = block >= 0

        @pl.when(held & above)
        def _():
            up_copy(k, block, seq + 2, k + 1).wait_send()

        @pl.when((held & (core == 0)) if k == 0 else held)
        def _():
            pair_copy(k, block).wait_send()


def per_device(
    query_rows, rotated_key_rows, value_row_matrix, group_assign, vertical_blocks, slash_offsets
):
    groups, seq_count = lax.axis_size("head"), lax.axis_size("seq")
    heads = QUERY_HEADS // groups
    kv_count = max(1, heads // SHARING)
    rows = query_rows.shape[0]
    seq_rows = rows * groups
    unit = math.gcd(rows, BLOCK_TOKENS)
    nv, ns = vertical_blocks.shape[1], slash_offsets.shape[1]
    chips = seq_count // 2
    pairs = heads * (seq_rows // BLOCK_TOKENS) * (nv + ns)
    dma = pltpu.SemaphoreType.DMA
    kind = query_rows.dtype

    def in_units(x):
        return x.reshape(rows // unit, unit, x.shape[1])

    attended = pl.pallas_call(
        functools.partial(fused_kernel, nv, ns),
        out_shape=jax.ShapeDtypeStruct((rows // unit, unit, query_rows.shape[1]), kind),
        in_specs=[pl.BlockSpec(memory_space=pltpu.SMEM)] * 3
        + [pl.BlockSpec(memory_space=pl.ANY)] * 3,
        out_specs=pl.BlockSpec(memory_space=pltpu.VMEM),
        scratch_shapes=[
            pltpu.VMEM((seq_rows // unit, unit, heads * HEAD_SIZE), kind),
            pltpu.VMEM((seq_rows * seq_count // unit, unit, 2 * kv_count * HEAD_SIZE), kind),
            pltpu.VMEM((heads, seq_rows // unit, unit, HEAD_SIZE), kind),
            pltpu.VMEM((QUERY_HEADS, rows // unit, unit, HEAD_SIZE), kind),
            dma((groups, 2)),
            dma((groups, 2)),
            dma((groups,)),
            dma((groups,)),
            dma((groups, heads)),
            dma((groups, heads)),
            dma((3,)),
            dma((heads,)),
            dma((chips,)),
            dma((chips + 1,)),
            dma((chips,)),
            dma((chips,)),
        ],
        compiler_params=pltpu.CompilerParams(
            collective_id=0, has_side_effects=True, vmem_limit_bytes=VMEM_BYTES
        ),
        cost_estimate=pl.CostEstimate(
            flops=pairs * 4 * BLOCK_TOKENS * BLOCK_TOKENS * HEAD_SIZE,
            bytes_accessed=2 * query_rows.nbytes + 2 * rotated_key_rows.nbytes,
            transcendentals=pairs * BLOCK_TOKENS * BLOCK_TOKENS,
        ),
    )(
        group_assign, vertical_blocks.reshape(-1), slash_offsets.reshape(-1),
        in_units(query_rows), in_units(rotated_key_rows), in_units(value_row_matrix),
    )
    return attended.reshape(query_rows.shape)


def solution(mesh):
    placed = (
        P(("seq", "head"), None),
        P(("seq", "head"), None),
        P(("seq", "head"), None),
        P(),
        P(),
        P(),
    )
    return jax.shard_map(
        per_device, mesh=mesh, in_specs=placed, out_specs=P(("seq", "head"), None), check_vma=False
    )
```

time: 170 us -> 103 us (0.61)
  the two profiles are of different devices: /device:TPU:0 before, /device:TPU:27 now
where the time goes in v2:
time: 103 us
  Pallas kernels  96.5 us (94%)
  local copies, waits for them, and re-layouts  6.39 us (6%)
    pallas_call x1, Pallas kernels, per_device(): pl.pallas_call(functools.partial(fused_kernel, nv, ns), out_shape=jax.Sha...  96.5 us
    unnamed x3, local copies, waits for them, and re-layouts  5.01 us

profile of v2, /device:TPU:27, one launch (start us, length us, event | category | flops | bytes accessed | tf_op | source)
XLA Modules:
  0.0 102.9 jit_solution(3802405304413588996)
XLA Ops:
  0.0 0.8 copy.7
  0.8 0.7 reshape.18.vert_ref
  1.4 0.8 copy.8
  2.2 0.7 reshape.19.slash_ref
  2.9 96.5 %shard_map.64 = bf16[5,32,8192]{2,1,0:T(8,128)(2,1)} custom-call(s32[64]{0:T(128)} %assign_ref.1, s32[256]{0:T(256)} %reshape.18.vert_ref, s32[192]{0:T(256)} %reshape.19.slash_ref, bf16[5,32,8192]{2,1,0:T(8,128)(2,1)} %bitcast.5, bf16[5,32,1024]{2,1,0:T(8,128)(2,1)} %bitcast.6, bf16[5,32,1024]{2,1,0:T(8,128)(2,1)} %bitcast.7), custom_call_target="tpu_custom_call" | custom-call | flops 4697620480 | bytes 5898240 | tf_op jit(solution)/shard_map/pallas_call | solution.py:330
  99.4 3.5 %copy.10 = bf16[160,8192]{1,0:T(8,128)(2,1)} copy(bf16[160,8192]{1,0:T(8,128)(2,1)} %bitcast.4) | data formatting | bytes 5242880

commit v3 on v2

--- a/solution.py
+++ b/solution.py
@@ -79,9 +79,9 @@
 
 def fused_kernel(
     nv, ns, assign_ref, vert_ref, slash_ref, query_ref, key_ref, value_ref, out_ref,
-    queries, keys_values, attended, received,
+    attended, received,
     kv_send, kv_recv, q_send, q_recv, o_send, o_recv, own_sem, mine_sem,
-    up_send, up_recv, pair_send, pair_recv,
+    up_send, up_recv, pair_send, pair_recv, *by_kv,
 ):
     groups, seq_count = lax.axis_size("head"), lax.axis_size("seq")
     group, seq = lax.axis_index("head"), lax.axis_index("seq")
@@ -90,10 +90,10 @@
     pair = seq + 1 - 2 * core
     resident, unit = query_ref.shape[:2]
     heads = QUERY_HEADS // groups
-    width = heads * HEAD_SIZE
-    kv_width = keys_values.shape[2] // 2
-    kv_count = kv_width // HEAD_SIZE
+    kv_count = len(by_kv) // 2
+    queries, keys_values = by_kv[:kv_count], by_kv[kv_count:]
     share = heads // kv_count
+    width = share * HEAD_SIZE
     seq_rows = resident * groups
     per_block = BLOCK_TOKENS // unit
     local_blocks = seq_rows // per_block
@@ -116,30 +116,32 @@
 
     pl.semaphore_wait(barrier, groups + above.astype(jnp.int32) + below.astype(jnp.int32))
 
-    def kv_columns(g):
-        first = lax.div(g * heads, SHARING) * HEAD_SIZE
-        return pl.ds(pl.multiple_of(first, HEAD_SIZE), kv_width)
+    def kv_columns(g, kv):
+        return columns_of(lax.div(g * heads, SHARING) + kv, HEAD_SIZE)
+
+    def half(part):
+        return pl.ds(part * HEAD_SIZE, HEAD_SIZE)
 
     def kv_rows(g):
         return pl.ds(seq * seq_rows + g * resident, resident)
 
-    def kv_copy(d, part, target, owner):
+    def kv_copy(d, kv, part, target, owner):
         source = (key_ref, value_ref)[part]
         return pltpu.make_async_remote_copy(
-            src_ref=source.at[:, :, kv_columns(target)],
-            dst_ref=keys_values.at[kv_rows(owner), :, pl.ds(part * kv_width, kv_width)],
-            send_sem=kv_send.at[d, part],
-            recv_sem=kv_recv.at[d, part],
+            src_ref=source.at[:, :, kv_columns(target, kv)],
+            dst_ref=keys_values[kv].at[kv_rows(owner), :, half(part)],
+            send_sem=kv_send.at[d, kv, part],
+            recv_sem=kv_recv.at[d, kv, part],
             device_id={"head": target},
             device_id_type=MESH,
         )
 
-    def q_copy(d, target, owner):
+    def q_copy(d, kv, target, owner):
         return pltpu.make_async_remote_copy(
-            src_ref=query_ref.at[:, :, columns_of(target, width)],
-            dst_ref=queries.at[units_of(owner, resident)],
-            send_sem=q_send.at[d],
-            recv_sem=q_recv.at[d],
+            src_ref=query_ref.at[:, :, columns_of(target * kv_count + kv, width)],
+            dst_ref=queries[kv].at[units_of(owner, resident)],
+            send_sem=q_send.at[d, kv],
+            recv_sem=q_recv.at[d, kv],
             device_id={"head": target},
             device_id_type=MESH,
         )
@@ -161,25 +163,25 @@
             mine_sem.at[h],
         )
 
-    def block_rows(b):
-        return keys_values.at[units_of(b, seq_rows)]
-
-    def up_copy(k, block, target, sem):
+    def block_rows(kv, b):
+        return keys_values[kv].at[units_of(b, seq_rows)]
+
+    def up_copy(kv, k, block, target, sem):
         return pltpu.make_async_remote_copy(
-            src_ref=block_rows(block),
-            dst_ref=block_rows(block),
-            send_sem=up_send.at[k],
-            recv_sem=up_recv.at[sem],
+            src_ref=block_rows(kv, block),
+            dst_ref=block_rows(kv, block),
+            send_sem=up_send.at[kv, k],
+            recv_sem=up_recv.at[kv, sem],
             device_id={"seq": target},
             device_id_type=MESH,
         )
 
-    def pair_copy(k, block):
+    def pair_copy(kv, k, block):
         return pltpu.make_async_remote_copy(
-            src_ref=block_rows(block),
-            dst_ref=block_rows(block),
-            send_sem=pair_send.at[k],
-            recv_sem=pair_recv.at[k],
+            src_ref=block_rows(kv, block),
+            dst_ref=block_rows(kv, block),
+            send_sem=pair_send.at[kv, k],
+            recv_sem=pair_recv.at[kv, k],
             device_id={"seq": pair},
             device_id_type=MESH,
         )
@@ -190,79 +192,103 @@
     def before(d):
         return lax.rem(group + groups - d, groups)
 
-    for d in range(1, groups):
-        for part in range(2):
-            kv_copy(d, part, later(d), group).start()
-    own = [
+    own_kv = [
+        [
+            pltpu.make_async_copy(
+                source.at[:, :, kv_columns(group, kv)],
+                keys_values[kv].at[kv_rows(group), :, half(part)],
+                own_sem.at[kv, part],
+            )
+            for part, source in enumerate((key_ref, value_ref))
+        ]
+        for kv in range(kv_count)
+    ]
+    own_q = [
         pltpu.make_async_copy(
-            source.at[:, :, kv_columns(group)],
-            keys_values.at[kv_rows(group), :, pl.ds(part * kv_width, kv_width)],
-            own_sem.at[part],
-        )
-        for part, source in enumerate((key_ref, value_ref))
+            query_ref.at[:, :, columns_of(group * kv_count + kv, width)],
+            queries[kv].at[units_of(group, resident)],
+            own_sem.at[kv, 2],
+        )
+        for kv in range(kv_count)
     ]
-    own.append(
-        pltpu.make_async_copy(
-            query_ref.at[:, :, columns_of(group, width)],
-            queries.at[units_of(group, resident)],
-            own_sem.at[2],
-        )
-    )
-    for copy in own:
-        copy.start()
-    for d in range(1, groups):
-        q_copy(d, later(d), group).start()
-    own[0].wait()
-    own[1].wait()
-    for d in range(1, groups):
-        for part in range(2):
-            kv_copy(d, part, group, before(d)).wait_recv()
-
-    for k in range(chips):
+
+    def send_kv(kv):
+        for d in range(1, groups):
+            for part in range(2):
+                kv_copy(d, kv, part, later(d), group).start()
+        for copy in own_kv[kv]:
+            copy.start()
+
+    def await_kv(kv):
+        for copy in own_kv[kv]:
+            copy.wait()
+        for d in range(1, groups):
+            for part in range(2):
+                kv_copy(d, kv, part, group, before(d)).wait_recv()
+
+    def send_q(kv):
+        for d in range(1, groups):
+            q_copy(d, kv, later(d), group).start()
+        own_q[kv].start()
+
+    def chain_step(kv, k):
         block = seq - 2 * k
         held = block >= 0
-
         if k:
 
             @pl.when(held)
             def _():
-                up_copy(k, block, seq, k).wait_recv()
+                up_copy(kv, k, block, seq, k).wait_recv()
 
         @pl.when(held & above)
         def _():
-            up_copy(k, block, seq + 2, k + 1).start()
+            up_copy(kv, k, block, seq + 2, k + 1).start()
 
         @pl.when((held & (core == 0)) if k == 0 else held)
         def _():
-            pair_copy(k, block).start()
-
-    for k in range(chips):
-        arrives = (core == 1) if k == 0 else pair - 2 * k >= 0
-
-        @pl.when(arrives)
-        def _():
-            pair_copy(k, pair - 2 * k).wait_recv()
-
-    own[2].wait()
-    for d in range(1, groups):
-        q_copy(d, group, before(d)).wait_recv()
+            pair_copy(kv, k, block).start()
+
+    send_kv(0)
+    await_kv(0)
+    chain_step(0, 0)
+    for kv in range(1, kv_count):
+        send_kv(kv)
+    send_q(0)
+    for k in range(1, chips):
+        chain_step(0, k)
+        if k == 1:
+            for kv in range(1, kv_count):
+                send_q(kv)
 
     for kv in range(kv_count):
-        key_column = kv * HEAD_SIZE
+        following = kv + 1
+        if following < kv_count:
+            await_kv(following)
+            chain_step(following, 0)
+        for k in range(chips):
+            arrives = (core == 1) if k == 0 else pair - 2 * k >= 0
+
+            @pl.when(arrives)
+            def _():
+                pair_copy(kv, k, pair - 2 * k).wait_recv()
+
+        own_q[kv].wait()
+        for d in range(1, groups):
+            q_copy(d, kv, group, before(d)).wait_recv()
 
         def one_head(j, carry):
             h = kv * share + j
             head = group * heads + h
             offsets = [slash_ref[head * ns + n] for n in range(ns)]
             verticals = [vert_ref[head * nv + n] for n in range(nv)]
-            column = columns_of(h, HEAD_SIZE)
+            column = columns_of(j, HEAD_SIZE)
             for n in range(local_blocks):
                 part = pl.ds(n * per_block, per_block)
                 blended = block_attention(
-                    queries[part, :, column].reshape(BLOCK_TOKENS, HEAD_SIZE),
-                    keys_values,
-                    key_column,
-                    kv_width + key_column,
+                    queries[kv][part, :, column].reshape(BLOCK_TOKENS, HEAD_SIZE),
+                    keys_values[kv],
+                    0,
+                    HEAD_SIZE,
                     seq * local_blocks + n,
                     offsets,
                     verticals,
@@ -271,6 +297,13 @@
             for d in range(1, groups):
                 o_copy(d, h, later(d), group).start()
             mine_copy(h).start()
+            if following < kv_count:
+                for k in range(1, chips):
+
+                    @pl.when(j == min(share, 2 + 2 * k) - 1)
+                    def _():
+                        chain_step(following, k)
+
             return carry
 
         lax.fori_loop(0, share, one_head, 0)
@@ -292,21 +325,22 @@
         return carry
 
     lax.fori_loop(0, heads, sent, 0)
-    for d in range(1, groups):
-        q_copy(d, later(d), group).wait_send()
-        for part in range(2):
-            kv_copy(d, part, later(d), group).wait_send()
-    for k in range(chips):
-        block = seq - 2 * k
-        held = block >= 0
-
-        @pl.when(held & above)
-        def _():
-            up_copy(k, block, seq + 2, k + 1).wait_send()
-
-        @pl.when((held & (core == 0)) if k == 0 else held)
-        def _():
-            pair_copy(k, block).wait_send()
+    for kv in range(kv_count):
+        for d in range(1, groups):
+            q_copy(d, kv, later(d), group).wait_send()
+            for part in range(2):
+                kv_copy(d, kv, part, later(d), group).wait_send()
+        for k in range(chips):
+            block = seq - 2 * k
+            held = block >= 0
+
+            @pl.when(held & above)
+            def _():
+                up_copy(kv, k, block, seq + 2, k + 1).wait_send()
+
+            @pl.when((held & (core == 0)) if k == 0 else held)
+            def _():
+                pair_copy(kv, k, block).wait_send()
 
 
 def per_device(
@@ -334,23 +368,23 @@
         + [pl.BlockSpec(memory_space=pl.ANY)] * 3,
         out_specs=pl.BlockSpec(memory_space=pltpu.VMEM),
         scratch_shapes=[
-            pltpu.VMEM((seq_rows // unit, unit, heads * HEAD_SIZE), kind),
-            pltpu.VMEM((seq_rows * seq_count // unit, unit, 2 * kv_count * HEAD_SIZE), kind),
             pltpu.VMEM((heads, seq_rows // unit, unit, HEAD_SIZE), kind),
             pltpu.VMEM((QUERY_HEADS, rows // unit, unit, HEAD_SIZE), kind),
-            dma((groups, 2)),
-            dma((groups, 2)),
-            dma((groups,)),
-            dma((groups,)),
+            dma((groups, kv_count, 2)),
+            dma((groups, kv_count, 2)),
+            dma((groups, kv_count)),
+            dma((groups, kv_count)),
             dma((groups, heads)),
             dma((groups, heads)),
-            dma((3,)),
+            dma((kv_count, 3)),
             dma((heads,)),
-            dma((chips,)),
-            dma((chips + 1,)),
-            dma((chips,)),
-            dma((chips,)),
-        ],
+            dma((kv_count, chips)),
+            dma((kv_count, chips + 1)),
+            dma((kv_count, chips)),
+            dma((kv_count, chips)),
+        ]
+        + [pltpu.VMEM((seq_rows // unit, unit, heads // kv_count * HEAD_SIZE), kind)] * kv_count
+        + [pltpu.VMEM((seq_rows * seq_count // unit, unit, 2 * HEAD_SIZE), kind)] * kv_count,
         compiler_params=pltpu.CompilerParams(
             collective_id=0, has_side_effects=True, vmem_limit_bytes=VMEM_BYTES
         ),

time: 103 us -> 85 us (0.83)
  Pallas kernels: 96.5 us -> 78.1 us
    pallas_call x1, Pallas kernels: 96.5 us -> 78.1 us  [per_device(): pl.pallas_call(functools.partial(fused_kernel, nv, ns), out_shape=jax.Sha...]
where the time goes in v3:
time: 85 us; the launch traced here: 84.5 us
  Pallas kernels  78.1 us (92%)
  local copies, waits for them, and re-layouts  6.39 us (8%)
    pallas_call x1, Pallas kernels, per_device(): pl.pallas_call(functools.partial(fused_kernel, nv, ns), out_shape=jax.Sha...  78.1 us
    unnamed x3, local copies, waits for them, and re-layouts  5.01 us

profile of v3, /device:TPU:27, one launch (start us, length us, event | category | flops | bytes accessed | tf_op | source)
XLA Modules:
  0.0 84.5 jit_solution(6331982219602960523)
XLA Ops:
  0.0 0.8 copy.7
  0.8 0.7 reshape.18.vert_ref
  1.4 0.8 copy.8
  2.2 0.7 reshape.19.slash_ref
  2.9 78.1 %shard_map.64 = bf16[5,32,8192]{2,1,0:T(8,128)(2,1)} custom-call(s32[64]{0:T(128)} %assign_ref.1, s32[256]{0:T(256)} %reshape.18.vert_ref, s32[192]{0:T(256)} %reshape.19.slash_ref, bf16[5,32,8192]{2,1,0:T(8,128)(2,1)} %bitcast.5, bf16[5,32,1024]{2,1,0:T(8,128)(2,1)} %bitcast.6, bf16[5,32,1024]{2,1,0:T(8,128)(2,1)} %bitcast.7), custom_call_target="tpu_custom_call" | custom-call | flops 4697620480 | bytes 5898240 | tf_op jit(solution)/shard_map/pallas_call | solution.py:364
  81.0 3.5 %copy.10 = bf16[160,8192]{1,0:T(8,128)(2,1)} copy(bf16[160,8192]{1,0:T(8,128)(2,1)} %bitcast.4) | data formatting | bytes 5242880
